TPU v7x, 32 devices: a whole 2x2x4 slice. The times are simulated.
32 devices in a mesh: grp: 2 (over x), seq: 8 (over z, y), dp: 2 (over core).
Axes of the slice: x: 2, y: 2, z: 4, core: 2. Of those that a mesh axis runs over, the one named last changes fastest.
Arguments:
- dec_query: bfloat16 [4, 1024, 2048], P(('grp', 'dp'), 'seq'), parts along dimension 0, may hold values from -9 to 9
- enc_key: bfloat16 [4, 4096, 2048], P(('grp', 'dp'), 'seq'), parts along dimension 0, may hold values from -4 to 4
- enc_value: bfloat16 [4, 4096, 2048], P(('grp', 'dp'), 'seq'), parts along dimension 0, may hold values from -6 to 6
- saved_out: bfloat16 [4, 1024, 2048], P(('grp', 'dp'), 'seq'), parts along dimension 0, may hold values from -3 to 3
- d_out: bfloat16 [4, 1024, 2048], P(('grp', 'dp'), 'seq'), parts along dimension 0, may hold values from -24 to 24
- dec_start: int32 [4, 33], P(('grp', 'dp')), parts along dimension 0, may hold values from 0 to 1024, as said below
- enc_start: int32 [4, 33], P(('grp', 'dp')), parts along dimension 0, may hold values from 0 to 4096, as said below
Outputs:
- d_query: bfloat16 [4, 1024, 2048], P(('grp', 'dp'), 'seq'), parts along dimension 0
- d_key: bfloat16 [4, 4096, 2048], P(('grp', 'dp'), 'seq'), parts along dimension 0
- d_value: bfloat16 [4, 4096, 2048], P(('grp', 'dp'), 'seq'), parts along dimension 0
There are 2 independent parts, one for each index of `grp`. A program takes and returns all parts, laid end to end along the dimension named above; each array names one. Nothing has to cross between parts.
Inputs may be any that keep to these rules, and one draw needn't show every extreme that they name: dec_start[b, 0] = 0 and dec_start[b, 32] = 1024; dec_start[b, k] = k * 32 plus a whole number from 0 to 16, so an example has 16 to 48 decoder tokens, and in every batch one example has exactly 48. enc_start[b, 0] = 0 and enc_start[b, 32] = 4096; enc_start[b, k] = k * 4 * 32 plus a whole number from 0 to 64, so an example has 64 to 192 encoder tokens, and in every batch one example has exactly 192.
All inputs are finite; a program needn't handle non-finite values.
Results may differ from a plain program's by a relative error of at most 0.005.
Values may be sent and summed in bfloat16 or wider, within the bound.
A program may use at most 128 MiB of HBM per device.

v0:
```python
import jax
import jax.numpy as jnp
from jax import lax
from jax.sharding import PartitionSpec as P

H = 32
HD = 64
REACH = 128


masked_low = -1e30


def extended(cells, sides, width):
    for axis, dim in sides:
        count = lax.axis_size(axis)
        ends = count - 1
        head = lax.slice_in_dim(cells, 0, width, axis=dim)
        tail = lax.slice_in_dim(cells, cells.shape[dim] - width, cells.shape[dim], axis=dim)
        cells = jnp.concatenate(
            [
                lax.ppermute(tail, axis, [(i, (i + 1) % count) for i in range(ends)]),
                cells,
                lax.ppermute(head, axis, [((i + 1) % count, i) for i in range(ends)]),
            ],
            axis=dim,
        )
    return cells


def from_behind(shard, axis, by):
    devices = lax.axis_size(axis)
    pairs = [(i, i + by) for i in range(devices) if 0 <= i + by < devices]
    return lax.ppermute(shard, axis, pairs)


def example_ids(positions, starts, total):
    counts = jnp.sum((positions[:, None] >= starts[None, 1:-1]).astype(jnp.int32), axis=1)
    inside = (positions >= 0) & (positions < total)
    return jnp.where(inside, counts, -1)


def shards(dec_query, enc_key, enc_value, saved_out, d_out, dec_start, enc_start):
    q_rows = dec_query.shape[1]
    k_rows = enc_key.shape[1]
    row_width = dec_query.shape[2]
    head_count = H
    head_dim = HD
    seq_pos = lax.axis_index("seq")
    seq_count = lax.axis_size("seq")
    block_rows = 128
    rim_rows = -(-REACH // block_rows) * block_rows
    stacked = jnp.stack([enc_key[0], enc_value[0]])
    window = extended(stacked, (("seq", 1),), rim_rows)
    window_rows = k_rows + 2 * rim_rows
    n_blocks = window_rows // block_rows
    key_pos = seq_pos * k_rows - rim_rows + jnp.arange(window_rows, dtype=jnp.int32)
    key_ids = example_ids(key_pos, enc_start[0], seq_count * k_rows)
    query_pos = seq_pos * q_rows + jnp.arange(q_rows, dtype=jnp.int32)
    query_ids = example_ids(query_pos, dec_start[0], seq_count * q_rows)
    queries = dec_query[0].reshape(q_rows, head_count, head_dim)
    grads_out = d_out[0].reshape(q_rows, head_count, head_dim)
    outputs = saved_out[0].reshape(q_rows, head_count, head_dim)
    out_dot = jnp.sum(grads_out.astype(jnp.float32) * outputs.astype(jnp.float32), axis=2).T

    def key_block(block_idx):
        row_start = block_idx * block_rows
        keys_blk = lax.dynamic_slice_in_dim(window[0], row_start, block_rows, 0).reshape(
            block_rows, head_count, head_dim
        )
        values_blk = lax.dynamic_slice_in_dim(window[1], row_start, block_rows, 0).reshape(
            block_rows, head_count, head_dim
        )
        ids_blk = lax.dynamic_slice_in_dim(key_ids, row_start, block_rows, 0)
        allowed = query_ids[:, None] == ids_blk[None, :]
        return (keys_blk, values_blk, allowed)

    def stats_step(running, block_idx):
        keys_blk, values_blk, allowed = key_block(block_idx)
        prev_max, prev_sum = running
        scores = jnp.einsum("qhd,khd->hqk", queries, keys_blk, preferred_element_type=jnp.float32)
        masked = jnp.where(allowed[None], scores, masked_low)
        new_max = jnp.maximum(prev_max, jnp.max(masked, axis=2))
        weights = jnp.where(allowed[None], jnp.exp(masked - new_max[:, :, None]), 0.0)
        result = (new_max, prev_sum * jnp.exp(prev_max - new_max) + jnp.sum(weights, axis=2))
        return (result, None)

    start_stats = (
        jnp.full((head_count, q_rows), masked_low, jnp.float32),
        jnp.zeros((head_count, q_rows), jnp.float32),
    )
    (row_max, row_sum), _ = lax.scan(stats_step, start_stats, jnp.arange(n_blocks, dtype=jnp.int32))
    log_total = row_max + jnp.log(row_sum)

    def grad_step(dq_total, block_idx):
        keys_blk, values_blk, allowed = key_block(block_idx)
        scores = jnp.einsum("qhd,khd->hqk", queries, keys_blk, preferred_element_type=jnp.float32)
        masked = jnp.where(allowed[None], scores, masked_low)
        weights = jnp.where(allowed[None], jnp.exp(masked - log_total[:, :, None]), 0.0)
        weights_low = weights.astype(jnp.bfloat16)
        d_probs = jnp.einsum(
            "qhd,khd->hqk", grads_out, values_blk, preferred_element_type=jnp.float32
        )
        d_scores = (weights * (d_probs - out_dot[:, :, None])).astype(jnp.bfloat16)
        dq_new = dq_total + jnp.einsum(
            "hqk,khd->qhd", d_scores, keys_blk, preferred_element_type=jnp.float32
        )
        dk_blk = jnp.einsum("hqk,qhd->khd", d_scores, queries, preferred_element_type=jnp.float32)
        dv_blk = jnp.einsum(
            "hqk,qhd->khd", weights_low, grads_out, preferred_element_type=jnp.float32
        )
        return (
            dq_new,
            jnp.stack(
                [dk_blk.reshape(block_rows, row_width), dv_blk.reshape(block_rows, row_width)]
            ),
        )

    start_query = jnp.zeros((q_rows, head_count, head_dim), jnp.float32)
    dq_final, pieces = lax.scan(grad_step, start_query, jnp.arange(n_blocks, dtype=jnp.int32))
    rim_blocks = rim_rows // block_rows
    own_blocks = k_rows // block_rows
    left_part = pieces[:rim_blocks]
    own_part = pieces[rim_blocks : rim_blocks + own_blocks]
    right_part = pieces[rim_blocks + own_blocks :]
    from_next = from_behind(left_part, "seq", -1)
    from_prev = from_behind(right_part.astype(jnp.bfloat16), "seq", 1).astype(right_part.dtype)
    filler = jnp.zeros((own_blocks - rim_blocks, 2, block_rows, row_width), jnp.float32)
    summed = (
        own_part
        + jnp.concatenate([from_prev, filler], axis=0)
        + jnp.concatenate([filler, from_next], axis=0)
    )
    grad_key = summed[:, 0].reshape(k_rows, row_width).astype(jnp.bfloat16)[None]
    grad_value = summed[:, 1].reshape(k_rows, row_width).astype(jnp.bfloat16)[None]
    grad_query = dq_final.reshape(q_rows, row_width).astype(jnp.bfloat16)[None]
    return (grad_query, grad_key, grad_value)


def solution(mesh):
    return jax.shard_map(
        shards,
        mesh=mesh,
        in_specs=(
            P(("grp", "dp"), "seq", None),
            P(("grp", "dp"), "seq", None),
            P(("grp", "dp"), "seq", None),
            P(("grp", "dp"), "seq", None),
            P(("grp", "dp"), "seq", None),
            P(("grp", "dp"), None),
            P(("grp", "dp"), None),
        ),
        out_specs=(
            P(("grp", "dp"), "seq", None),
            P(("grp", "dp"), "seq", None),
            P(("grp", "dp"), "seq", None),
        ),
        check_vma=False,
    )
```

profile of v0, /device:TPU:0, one launch (start us, length us, event | category | flops | bytes accessed | tf_op | source)
XLA Modules:
  0.0 241.6 jit_solution(860510484492957975)
XLA Ops:
  0.6 2.9 %copy.35 = bf16[1,512,2048]{1,2,0:T(8,128)(2,1)S(1)} copy(bf16[1,512,2048]{2,1,0:T(8,128)(2,1)} %param.12) | data formatting | bytes 4194304 | tf_op args[1]
  3.5 4.6 %copy.36 = bf16[1,512,2048]{1,2,0:T(8,128)(2,1)} copy(bf16[1,512,2048]{2,1,0:T(8,128)(2,1)} %param.13) | data formatting | bytes 4194304 | tf_op args[2]
  8.1 2.9 %pad_maximum_fusion.2 = (bf16[2,128,2048]{1,2,0:T(8,128)(2,1)}, bf16[2,128,2048]{1,2,0:T(8,128)(2,1)}) fusion(bf16[1,512,2048]{1,2,0:T(8,128)(2,1)} %copy.36, bf16[1,512,2048]{1,2,0:T(8,128)(2,1)S(1)} %copy.35), kind=kLoop, calls=%fused_computation.27 | loop fusion | flops 4194304 | bytes 6291456 | tf_op jit(solution)/shard_map/slice | solution.py:19
  11.0 6.0 %collective-permute-start = (bf16[2,128,2048]{1,2,0:T(8,128)(2,1)}, bf16[2,128,2048]{1,2,0:T(8,128)(2,1)}, u32[]{:S(2)}, u32[]{:S(2)}) collective-permute-start(bf16[2,128,2048]{1,2,0:T(8,128)(2,1)} %get-tuple-element.223), channel_id=1, source_target_pairs={{0,2},{2,4},{4,6},{6,8},{8,10},{10,12},{12,14},{1,3},{3,5},{5,7},{... | collective-permute-start | bytes 3145736 | tf_op jit(solution)/shard_map/ppermute | solution.py:22
  20.7 40.5 %collective-permute-done = bf16[2,128,2048]{1,2,0:T(8,128)(2,1)} collective-permute-done((bf16[2,128,2048]{1,2,0:T(8,128)(2,1)}, bf16[2,128,2048]{1,2,0:T(8,128)(2,1)}, u32[]{:S(2)}, u32[]{:S(2)}) %collective-permute-start) | collective-permute-done | bytes 1048608 | tf_op jit(solution)/shard_map/ppermute | solution.py:22
  61.2 6.4 %pad_maximum_fusion = bf16[2,768,2048]{1,2,0:T(8,128)(2,1)} fusion(bf16[2,128,2048]{1,2,0:T(8,128)(2,1)} %collective-permute-done.1, bf16[1,512,2048]{1,2,0:T(8,128)(2,1)} %copy.36, bf16[1,512,2048]{1,2,0:T(8,128)(2,1)} %copy-done, bf16[2,128,2048]{1,2,0:T(8,128)(2,1)} %collective-permute-done), kind=kLoop, calls=%fused_computation.24 | loop fusion | flops 25165824 | bytes 12582912 | tf_op jit(solution)/shard_map/concatenate | solution.py:20
  67.6 27.7 %while.26 = (s32[]{:T(128)}, f32[32,128]{1,0:T(8,128)S(1)}, f32[32,128]{1,0:T(8,128)S(1)}, s32[128]{0:T(128)S(1)}, s32[6]{0:T(128)S(1)}, /*index=5*/s32[768]{0:T...) while((s32[]{:T(128)}, f32[32,128]{1,0:T(8,128)S(1)}, ...), condition=%wide.region_5.6_spmd.clone, body=%wide.region_2.0_spmd.clone.sunk | while | flops 70291464 | bytes 12847306 | solution.py:92
  69.0 2.1 slice.68
  73.6 2.1 slice.68
  82.9 2.1 slice.68
  87.5 2.1 slice.68
  95.3 57.7 %while.27 = (s32[]{:T(128)}, f32[128,32,64]{0,2,1:T(8,128)S(1)}, f32[6,2,128,2048]{2,3,1,0:T(8,128)}, bf16[2,768,2048]{1,2,0:T(8,128)(2,1)}, s32[6]{0:T(128)S(1)...) while((s32[]{:T(128)}, f32[128,32,64]{0,2,1:T(8,128)S(1)}, ...), condition=%wide.region_8.9_spmd.clone, body=%wide.region_7.8_spmd.clone.sunk | while | flops 340279296 | bytes 36243684 | solution.py:120
  96.7 3.3 %fusion.59 = (bf16[1,768,2048]{1,2,0:T(8,128)(2,1)S(1)}, bf16[1,768,2048]{1,2,0:T(8,128)(2,1)S(1)}) fusion(bf16[2,768,2048]{1,2,0:T(8,128)(2,1)} %get-tuple-element.422), kind=kLoop, calls=%fused_computation.38.clone.1 | loop fusion | bytes 12582912 | tf_op jit(solution)/shard_map/while/body/eval_jaxpr/slice | solution.py:71
  106.4 3.3 %fusion.59 = (bf16[1,768,2048]{1,2,0:T(8,128)(2,1)S(1)}, bf16[1,768,2048]{1,2,0:T(8,128)(2,1)S(1)}) fusion(bf16[2,768,2048]{1,2,0:T(8,128)(2,1)} %get-tuple-element.422), kind=kLoop, calls=%fused_computation.38.clone.1 | loop fusion | bytes 12582912 | tf_op jit(solution)/shard_map/while/body/eval_jaxpr/slice | solution.py:71
  115.9 3.3 %fusion.59 = (bf16[1,768,2048]{1,2,0:T(8,128)(2,1)S(1)}, bf16[1,768,2048]{1,2,0:T(8,128)(2,1)S(1)}) fusion(bf16[2,768,2048]{1,2,0:T(8,128)(2,1)} %get-tuple-element.422), kind=kLoop, calls=%fused_computation.38.clone.1 | loop fusion | bytes 12582912 | tf_op jit(solution)/shard_map/while/body/eval_jaxpr/slice | solution.py:71
  125.5 3.3 %fusion.59 = (bf16[1,768,2048]{1,2,0:T(8,128)(2,1)S(1)}, bf16[1,768,2048]{1,2,0:T(8,128)(2,1)S(1)}) fusion(bf16[2,768,2048]{1,2,0:T(8,128)(2,1)} %get-tuple-element.422), kind=kLoop, calls=%fused_computation.38.clone.1 | loop fusion | bytes 12582912 | tf_op jit(solution)/shard_map/while/body/eval_jaxpr/slice | solution.py:71
  135.2 3.3 %fusion.59 = (bf16[1,768,2048]{1,2,0:T(8,128)(2,1)S(1)}, bf16[1,768,2048]{1,2,0:T(8,128)(2,1)S(1)}) fusion(bf16[2,768,2048]{1,2,0:T(8,128)(2,1)} %get-tuple-element.422), kind=kLoop, calls=%fused_computation.38.clone.1 | loop fusion | bytes 12582912 | tf_op jit(solution)/shard_map/while/body/eval_jaxpr/slice | solution.py:71
  144.8 3.3 %fusion.59 = (bf16[1,768,2048]{1,2,0:T(8,128)(2,1)S(1)}, bf16[1,768,2048]{1,2,0:T(8,128)(2,1)S(1)}) fusion(bf16[2,768,2048]{1,2,0:T(8,128)(2,1)} %get-tuple-element.422), kind=kLoop, calls=%fused_computation.38.clone.1 | loop fusion | bytes 12582912 | tf_op jit(solution)/shard_map/while/body/eval_jaxpr/slice | solution.py:71
  153.0 3.0 %slice.47 = f32[1,2,128,2048]{2,3,1,0:T(8,128)} slice(f32[6,2,128,2048]{2,3,1,0:T(8,128)} %get-tuple-element.107), slice={[0:1], [0:2], [0:128], [0:2048]} | slice | bytes 4194304 | tf_op jit(solution)/shard_map/slice | solution.py:123
  159.1 6.0 %collective-permute-start.2 = (bf16[1,2,128,2048]{2,3,1,0:T(8,128)(2,1)S(1)}, bf16[1,2,128,2048]{2,3,1,0:T(8,128)(2,1)}, u32[]{:S(2)}, u32[]{:S(2)}) collective-permute-start(bf16[1,2,128,2048]{2,3,1,0:T(8,128)(2,1)S(1)} %slice.60), channel_id=1, source_target_pairs={{0,2},{2,4},{4,6},{6,8},{8,10},{10,12},{12,14},{1,3},{3,5},{5,7},{... | collective-permute-start | bytes 3145736 | tf_op jit(solution)/shard_map/ppermute | solution.py:34
  166.2 62.7 %collective-permute-done.2 = bf16[1,2,128,2048]{2,3,1,0:T(8,128)(2,1)} collective-permute-done((bf16[1,2,128,2048]{2,3,1,0:T(8,128)(2,1)S(1)}, bf16[1,2,128,2048]{2,3,1,0:T(8,128)(2,1)}, u32[]{:S(2)}, u32[]{:S(2)}) %collective-permute-start.2) | collective-permute-done | bytes 1048608 | tf_op jit(solution)/shard_map/ppermute | solution.py:34
  228.8 4.6 %add_convert_fusion = bf16[4,2,128,2048]{2,3,1,0:T(8,128)(2,1)S(1)} fusion(f32[1,2,128,2048]{2,3,1,0:T(8,128)} %collective-permute-done.3, f32[6,2,128,2048]{2,3,1,0:T(8,128)} %get-tuple-element.107, bf16[1,2,128,2048]{2,3,1,0:T(8,128)(2,1)} %collective-permute-done.2), kind=kLoop, calls=%fused_computation.23 | loop fusion | flops 8388608 | bytes 15728640 | tf_op jit(solution)/shard_map/convert.4
  235.1 3.9 %copy.41 = bf16[4,1,128,2048]{3,2,0,1:T(8,128)(2,1)} copy(bf16[4,1,128,2048]{2,3,1,0:T(8,128)(2,1)} %get-tuple-element.221) | data formatting | bytes 4194304 | tf_op jit(solution)/shard_map/slice | solution.py:135
  239.0 2.6 %copy.40 = bf16[4,1,128,2048]{3,2,0,1:T(8,128)(2,1)} copy(bf16[4,1,128,2048]{2,3,1,0:T(8,128)(2,1)S(1)} %get-tuple-element.222) | data formatting | bytes 4194304 | tf_op jit(solution)/shard_map/slice | solution.py:134
  (153 shorter events, 58.3 us)
Async XLA Ops:
  3.5 4.6 %copy-start = (bf16[1,512,2048]{1,2,0:T(8,128)(2,1)}, bf16[1,512,2048]{1,2,0:T(8,128)(2,1)S(1)}, u32[]{:S(2)}) copy-start(bf16[1,512,2048]{1,2,0:T(8,128)(2,1)S(1)} %copy.35) | copy-start | bytes 6291460
  8.1 10.2 %copy-start.3 = (s32[1,33]{1,0:T(1,128)S(1)}, s32[1,33]{1,0:T(1,128)}, u32[]{:S(2)}) copy-start(s32[1,33]{1,0:T(1,128)} %param.16) | copy-start | bytes 400
  8.1 10.3 %copy-start.1 = (bf16[1,128,2048]{2,1,0:T(8,128)(2,1)S(1)}, bf16[1,128,2048]{2,1,0:T(8,128)(2,1)}, u32[]{:S(2)}) copy-start(bf16[1,128,2048]{2,1,0:T(8,128)(2,1)} %param.11) | copy-start | bytes 1572868
  8.1 10.6 %copy-start.2 = (bf16[1,128,2048]{2,1,0:T(8,128)(2,1)S(1)}, bf16[1,128,2048]{2,1,0:T(8,128)(2,1)}, u32[]{:S(2)}) copy-start(bf16[1,128,2048]{2,1,0:T(8,128)(2,1)} %param.15) | copy-start | bytes 1572868
  11.0 9.3 %copy-start.4 = (s32[1,33]{1,0:T(1,128)S(1)}, s32[1,33]{1,0:T(1,128)}, u32[]{:S(2)}) copy-start(s32[1,33]{1,0:T(1,128)} %param.17) | copy-start | bytes 400
  11.0 50.2 %collective-permute-start = (bf16[2,128,2048]{1,2,0:T(8,128)(2,1)}, bf16[2,128,2048]{1,2,0:T(8,128)(2,1)}, u32[]{:S(2)}, u32[]{:S(2)}) collective-permute-start(bf16[2,128,2048]{1,2,0:T(8,128)(2,1)} %get-tuple-element.223), channel_id=1, source_target_pairs={{0,2},{2,4},{4,6},{6,8},{8,10},{10,12},{12,14},{1,3},{3,5},{5,7},{... | collective-permute-start | bytes 3145736 | tf_op jit(solution)/shard_map/ppermute | solution.py:22
  17.0 44.2 %collective-permute-start.1 = (bf16[2,128,2048]{1,2,0:T(8,128)(2,1)}, bf16[2,128,2048]{1,2,0:T(8,128)(2,1)}, u32[]{:S(2)}, u32[]{:S(2)}) collective-permute-start(bf16[2,128,2048]{1,2,0:T(8,128)(2,1)} %get-tuple-element.224), channel_id=1, source_target_pairs={{2,0},{4,2},{6,4},{8,6},{10,8},{12,10},{14,12},{3,1},{5,3},{7,5},{... | collective-permute-start | bytes 3145736 | tf_op jit(solution)/shard_map/ppermute | solution.py:24
  156.0 72.8 %collective-permute-start.3 = (f32[1,2,128,2048]{2,3,1,0:T(8,128)}, f32[1,2,128,2048]{2,3,1,0:T(8,128)}, u32[]{:S(2)}, u32[]{:S(2)}) collective-permute-start(f32[1,2,128,2048]{2,3,1,0:T(8,128)} %slice.47), channel_id=1, source_target_pairs={{2,0},{4,2},{6,4},{8,6},{10,8},{12,10},{14,12},{3,1},{5,3},{7,5},{... | collective-permute-start | bytes 6291464 | tf_op jit(solution)/shard_map/ppermute | solution.py:34
  159.1 69.8 %collective-permute-start.2 = (bf16[1,2,128,2048]{2,3,1,0:T(8,128)(2,1)S(1)}, bf16[1,2,128,2048]{2,3,1,0:T(8,128)(2,1)}, u32[]{:S(2)}, u32[]{:S(2)}) collective-permute-start(bf16[1,2,128,2048]{2,3,1,0:T(8,128)(2,1)S(1)} %slice.60), channel_id=1, source_target_pairs={{0,2},{2,4},{4,6},{6,8},{8,10},{10,12},{12,14},{1,3},{3,5},{5,7},{... | collective-permute-start | bytes 3145736 | tf_op jit(solution)/shard_map/ppermute | solution.py:34
where the time goes:
time: 243 us; the launch traced here: 242 us
  waiting for transfers between devices  103 us (42%)
  local copies, waits for them, and re-layouts  64.1 us (26%)
  other arithmetic  27.2 us (11%)
  matrix products  23.2 us (10%)
  starting transfers between devices  14.6 us (6%)
  loops' own time  8.55 us (4%)
    ppermute x2, waiting for transfers between devices, from_behind(): return lax.ppermute(shard, axis, pairs)  62.7 us
    ppermute x1, waiting for transfers between devices, extended(): lax.ppermute(tail, axis, [(i, (i + 1) % count) for i in range(ends)])  40.5 us
    slice x6, local copies, waits for them, and re-layouts, key_block(): window[1]  19.5 us
    slice x6, local copies, waits for them, and re-layouts, key_block(): window[0]  12.6 us
    unnamed x15, local copies, waits for them, and re-layouts  9.03 us
    dynamic_update_slice x6, other arithmetic, shards(): lax.scan(grad_step, start_query, jnp.arange(n_blocks, dtype=jnp.int32))  8.86 us
    ppermute x2, starting transfers between devices, from_behind(): return lax.ppermute(shard, axis, pairs)  7.29 us
    dynamic_slice x12, local copies, waits for them, and re-layouts, shards(): lax.scan(stats_step, start_stats, jnp.arange(n_blocks, dtype=jnp.int32))  7.01 us
  transfers between devices with their start and end apart: 4, of which 2 were waited for; matrix products, arithmetic and copies ran while one was open for 2% of the time, Pallas kernels for 0%

commit v1 on v0

v1 whole, which is shorter than its diff:
```python
import functools

import jax
import jax.numpy as jnp
from jax import lax
from jax.experimental import pallas as pl
from jax.experimental.pallas import tpu as pltpu
from jax.sharding import PartitionSpec as P

HD = 64
WIDTH = 256
HPG = WIDTH // HD

masked_low = -1e30
NT = (((1,), (1,)), ((), ()))
TN = (((0,), (0,)), ((), ()))
NN = (((1,), (0,)), ((), ()))


def dot(a, b, dims):
    return lax.dot_general(a, b, dims, preferred_element_type=jnp.float32)


def kernel(
    n_seq, n_loc, step, enc_step,
    ds_ref, es_ref, q_hbm, k_hbm, v_hbm, so_hbm, do_hbm,
    dq_hbm, dk_hbm, dv_hbm,
    q, do, so, k, v, xq, xo, bdq, bdo, sbuf, dsb, psb, kid, st, rst_l, rst_r,
    dq, dqx, rdq_a, rdq_b, dqo, dk, dv,
    in_sem, snd, rcv, out_sem,
):
    me = lax.axis_index("seq")
    has_left = me > 0
    has_right = me < n_seq - 1
    q_rows = n_loc * step
    k_rows = n_loc * enc_step
    half = step // 2
    ehalf = enc_step // 2
    lanes = HPG * step
    groups = q.shape[1] // WIDTH
    last = n_loc + 1

    loads = [
        pltpu.make_async_copy(a.at[0], b, in_sem.at[n])
        for n, (a, b) in enumerate(((q_hbm, q), (k_hbm, k), (v_hbm, v), (do_hbm, do), (so_hbm, so)))
    ]
    for c in loads:
        c.start()

    xq[...] = jnp.zeros_like(xq)
    xo[...] = jnp.zeros_like(xo)
    for r in (rst_l, rst_r):
        r[...] = jnp.zeros_like(r)
        for n in range(2):
            r[n, 0] = jnp.full(r.shape[2:], masked_low, jnp.float32)
    rdq_a[...] = jnp.zeros_like(rdq_a)
    rdq_b[...] = jnp.zeros_like(rdq_b)

    barrier = pltpu.get_barrier_semaphore()

    def signal(to):
        pl.semaphore_signal(
            barrier, inc=1, device_id={"seq": to}, device_id_type=pl.DeviceIdType.MESH
        )

    pl.when(has_left)(lambda: signal(me - 1))
    pl.when(has_right)(lambda: signal(me + 1))
    pl.semaphore_wait(barrier, has_left.astype(jnp.int32) + has_right.astype(jnp.int32))

    def remote(src, dst, n, to):
        return pltpu.make_async_remote_copy(
            src_ref=src, dst_ref=dst, send_sem=snd.at[n], recv_sem=rcv.at[n],
            device_id={"seq": to}, device_id_type=pl.DeviceIdType.MESH,
        )

    tail = pl.ds(q_rows - step, step)
    head = pl.ds(0, half)
    to_right = [
        remote(q_hbm.at[0, tail], xq.at[pl.ds(0, step)], 0, me + 1),
        remote(do_hbm.at[0, tail], xo.at[pl.ds(0, step)], 1, me + 1),
        remote(st.at[pl.ds(last - 1, 2)], rst_l, 2, me + 1),
        remote(dqx.at[pl.ds(step, half)], rdq_a, 3, me + 1),
    ]
    to_left = [
        remote(q_hbm.at[0, head], xq.at[pl.ds(step, half)], 4, me - 1),
        remote(do_hbm.at[0, head], xo.at[pl.ds(step, half)], 5, me - 1),
        remote(st.at[pl.ds(0, 2)], rst_r, 6, me - 1),
        remote(dqx.at[pl.ds(0, step)], rdq_b, 7, me - 1),
    ]

    def start(ns):
        def right():
            for n in ns:
                to_right[n].start()

        def left():
            for n in ns:
                to_left[n].start()

        pl.when(has_right)(right)
        pl.when(has_left)(left)

    def arrived(ns):
        def from_left():
            for n in ns:
                to_right[n].wait_recv()

        def from_right():
            for n in ns:
                to_left[n].wait_recv()

        pl.when(has_left)(from_left)
        pl.when(has_right)(from_right)

    start((0, 1))

    def ids(pos, starts):
        total = jnp.zeros(pos.shape, jnp.int32)
        for t in range(-1, n_loc + 1):
            total += (pos >= starts[0, jnp.maximum(me * n_loc + t, 0)]).astype(jnp.int32)
        return total

    kid[...] = ids(me * k_rows + lax.broadcasted_iota(jnp.int32, (k_rows, lanes), 0), es_ref)
    lane_row = lax.rem(lax.broadcasted_iota(jnp.int32, (1, lanes), 1), step)
    qid = [ids(me * q_rows + (c - 1) * step + lane_row, ds_ref) for c in range(last + 1)]
    lane_head = lax.div(lax.broadcasted_iota(jnp.int32, (step, WIDTH), 1), HD)

    def spread(x):
        return jnp.concatenate(
            [jnp.where(lane_head == h, x, jnp.zeros_like(x)) for h in range(HPG)], axis=0
        )

    def gather(x):
        total = jnp.zeros((step, WIDTH), jnp.float32)
        for h in range(HPG):
            total = jnp.where(lane_head == h, x[h * step : (h + 1) * step], total)
        return total

    def rows_of(c):
        lo = max(0, (c - 2) * enc_step)
        hi = min(k_rows, c * enc_step + ehalf)
        return lo, hi

    s_at = {}
    at = 0
    for c in (0, 1, last - 1, last):
        s_at[c] = at
        at += rows_of(c)[1] - rows_of(c)[0]

    def cols(g):
        return pl.ds(pl.multiple_of(g * WIDTH, WIDTH), WIDTH)

    def blk(c):
        return pl.ds(c * lanes, lanes)

    def build(g, c, qs, dos):
        bdq[g, blk(c)] = spread(qs)
        bdo[g, blk(c)] = spread(dos)

    ones = jnp.ones((8, WIDTH), jnp.bfloat16)

    def out_dot(dos, sos):
        w = dos.astype(jnp.float32) * sos.astype(jnp.float32)
        hi = w.astype(jnp.bfloat16)
        rest = w - hi.astype(jnp.float32)
        mid = rest.astype(jnp.bfloat16)
        low = (rest - mid.astype(jnp.float32)).astype(jnp.bfloat16)
        total = dot(ones, spread(low), NT) + dot(ones, spread(mid), NT) + dot(ones, spread(hi), NT)
        return total[0:1]

    def scores(g, c):
        lo, hi = rows_of(c)
        s = dot(k[lo:hi, cols(g)], bdq[g, blk(c)], NT)
        s = jnp.where(kid[lo:hi] == qid[c], s, masked_low)
        m = jnp.max(s, axis=0, keepdims=True)
        l = jnp.sum(jnp.exp(s - jnp.maximum(m, 0.5 * masked_low)), axis=0, keepdims=True)
        return s, m, l

    def first_pass(g, c):
        s, m, l = scores(g, c)
        sbuf[g, pl.ds(s_at[c], s.shape[0])] = s
        st[c, 0, pl.ds(g, 1)] = m
        st[c, 1, pl.ds(g, 1)] = l

    def second_pass(g, c, s, total, od):
        lo, hi = rows_of(c)
        p = jnp.exp(s - total)
        dp = dot(v[lo:hi, cols(g)], bdo[g, blk(c)], NT)
        dsc = (p * (dp - od)).astype(jnp.bfloat16)
        psb[g, lo:hi, blk(c)] = p.astype(jnp.bfloat16)
        dsb[g, lo:hi, blk(c)] = dsc
        return gather(dot(dsc, k[lo:hi, cols(g)], TN))

    def own(c):
        return pl.ds((c - 1) * step, step)

    for c in loads:
        c.wait()

    @pl.loop(0, groups)
    def _(g):
        for j in range(n_loc):
            z = jnp.zeros((enc_step - ehalf, lanes), jnp.bfloat16)
            psb[g, pl.ds(j * enc_step + ehalf, enc_step - ehalf), blk(j)] = z
            dsb[g, pl.ds(j * enc_step + ehalf, enc_step - ehalf), blk(j)] = z
        for c in range(1, last):
            dos = do[own(c), cols(g)]
            build(g, c, q[own(c), cols(g)], dos)
            od = out_dot(dos, so[own(c), cols(g)])
            if c in (1, last - 1):
                first_pass(g, c)
                st[c, 2, pl.ds(g, 1)] = od
            else:
                s, m, l = scores(g, c)
                dq[own(c), cols(g)] = second_pass(g, c, s, m + jnp.log(l), od)

    arrived((0, 1))

    @pl.loop(0, groups)
    def _(g):
        for c in (0, last):
            r = pl.ds(0 if c == 0 else step, step)
            build(g, c, xq[r, cols(g)], xo[r, cols(g)])
            first_pass(g, c)
            st[c, 2, pl.ds(g, 1)] = jnp.zeros((1, lanes), jnp.float32)

    start((2,))
    arrived((2,))

    def finish(g, c, other, od_ref):
        row = pl.ds(g, 1)
        m1, m2 = st[c, 0, row], other[0, row]
        l1, l2 = st[c, 1, row], other[1, row]
        m = jnp.maximum(m1, m2)
        l = l1 * jnp.exp(m1 - m) + l2 * jnp.exp(m2 - m)
        total = jnp.where(l > 0.0, m + jnp.log(l), 0.0)
        lo, hi = rows_of(c)
        s = sbuf[g, pl.ds(s_at[c], hi - lo)]
        return second_pass(g, c, s, total, od_ref[2, row])

    @pl.loop(0, groups)
    def _(g):
        dqx[pl.ds(0, step), cols(g)] = finish(
            g, 0, rst_l.at[0], rst_l.at[0]).astype(jnp.bfloat16)
        dqx[pl.ds(step, step), cols(g)] = finish(
            g, last, rst_r.at[1], rst_r.at[1]).astype(jnp.bfloat16)

    start((3,))

    outs = []
    @pl.loop(0, groups)
    def _(g):
        dq[own(1), cols(g)] = finish(g, 1, rst_l.at[1], st.at[1])
        dq[own(last - 1), cols(g)] = finish(g, last - 1, rst_r.at[0], st.at[last - 1])
        for j in range(n_loc):
            rows = pl.ds(j * enc_step, enc_step)
            span = pl.ds(j * lanes, 3 * lanes)
            dk[rows, cols(g)] = dot(dsb[g, rows, span], bdq[g, span], NN).astype(jnp.bfloat16)
            dv[rows, cols(g)] = dot(psb[g, rows, span], bdo[g, span], NN).astype(jnp.bfloat16)
        pltpu.make_async_copy(dk.at[:, cols(g)], dk_hbm.at[0, :, cols(g)], out_sem.at[0, g]).start()
        pltpu.make_async_copy(dv.at[:, cols(g)], dv_hbm.at[0, :, cols(g)], out_sem.at[1, g]).start()

    arrived((3,))
    dq[pl.ds(0, half)] = dq[pl.ds(0, half)] + rdq_a[...].astype(jnp.float32)
    dq[tail] = dq[tail] + rdq_b[...].astype(jnp.float32)
    dqo[...] = dq[...].astype(jnp.bfloat16)
    fin = pltpu.make_async_copy(dqo, dq_hbm.at[0], in_sem.at[0])
    fin.start()

    @pl.loop(0, groups)
    def _(g):
        pltpu.make_async_copy(dk.at[:, cols(g)], dk_hbm.at[0, :, cols(g)], out_sem.at[0, g]).wait()
        pltpu.make_async_copy(dv.at[:, cols(g)], dv_hbm.at[0, :, cols(g)], out_sem.at[1, g]).wait()

    fin.wait()

    def sent_right():
        for c in to_right:
            c.wait_send()

    def sent_left():
        for c in to_left:
            c.wait_send()

    pl.when(has_right)(sent_right)
    pl.when(has_left)(sent_left)


def shards(dec_query, enc_key, enc_value, saved_out, d_out, dec_start, enc_start):
    n_seq = lax.axis_size("seq")
    _, q_rows, width = dec_query.shape
    k_rows = enc_key.shape[1]
    n_loc = (dec_start.shape[1] - 1) // n_seq
    step = q_rows // n_loc
    enc_step = k_rows // n_loc
    half = step // 2
    lanes = HPG * step
    groups = width // WIDTH
    chunks = n_loc + 2
    ehalf = enc_step // 2
    held = ehalf + (enc_step + ehalf) + 2 * enc_step + enc_step
    bf, f32 = jnp.bfloat16, jnp.float32
    vm = pltpu.VMEM
    hbm = pl.BlockSpec(memory_space=pl.ANY)
    smem = pl.BlockSpec(memory_space=pltpu.SMEM)
    return pl.pallas_call(
        functools.partial(kernel, n_seq, n_loc, step, enc_step),
        out_shape=(
            jax.ShapeDtypeStruct(dec_query.shape, bf),
            jax.ShapeDtypeStruct(enc_key.shape, bf),
            jax.ShapeDtypeStruct(enc_value.shape, bf),
        ),
        in_specs=[smem, smem] + [hbm] * 5,
        out_specs=(hbm, hbm, hbm),
        scratch_shapes=[
            vm((q_rows, width), bf), vm((q_rows, width), bf), vm((q_rows, width), bf),
            vm((k_rows, width), bf), vm((k_rows, width), bf),
            vm((2 * step, width), bf), vm((2 * step, width), bf),
            vm((groups, chunks * lanes, WIDTH), bf), vm((groups, chunks * lanes, WIDTH), bf),
            vm((groups, held, lanes), f32),
            vm((groups, k_rows, chunks * lanes), bf), vm((groups, k_rows, chunks * lanes), bf),
            vm((k_rows, lanes), jnp.int32),
            vm((chunks, 3, groups, lanes), f32),
            vm((2, 3, groups, lanes), f32), vm((2, 3, groups, lanes), f32),
            vm((q_rows, width), f32), vm((2 * step, width), bf),
            vm((half, width), bf), vm((step, width), bf), vm((q_rows, width), bf),
            vm((k_rows, width), bf), vm((k_rows, width), bf),
            pltpu.SemaphoreType.DMA((5,)),
            pltpu.SemaphoreType.DMA((8,)), pltpu.SemaphoreType.DMA((8,)),
            pltpu.SemaphoreType.DMA((2, groups)),
        ],
        compiler_params=pltpu.CompilerParams(
            collective_id=0, has_side_effects=True, vmem_limit_bytes=56 * 1024 * 1024
        ),
    )(dec_start, enc_start, dec_query, enc_key, enc_value, saved_out, d_out)


def solution(mesh):
    rows = P(("grp", "dp"), "seq", None)
    starts = P(("grp", "dp"), None)
    return jax.shard_map(
        shards,
        mesh=mesh,
        in_specs=(rows, rows, rows, rows, rows, starts, starts),
        out_specs=(rows, rows, rows),
        check_vma=False,
    )
```

time: 243 us -> 40.7 us (0.17)
  waiting for transfers between devices: 103 us -> 0 us
  local copies, waits for them, and re-layouts: 64.1 us -> 6.51 us
  Pallas kernels: 0 us -> 33.4 us
  other arithmetic: 27.2 us -> 0 us
  matrix products: 23.2 us -> 0 us
  starting transfers between devices: 14.6 us -> 0 us
  loops' own time: 8.55 us -> 0 us
    ppermute x4 -> x0, waiting for transfers between devices: 103 us -> none  [the longest x2 62.7 us: from_behind(): return lax.ppermute(shard, axis, pairs)]
    slice x17 -> x0, local copies, waits for them, and re-layouts: 45 us -> none  [the longest x6 19.5 us: key_block(): window[1]]
    pallas_call x0 -> x1, Pallas kernels: none -> 33.4 us  [shards(): pl.pallas_call(functools.partial(kernel, n_seq, n_loc, step, enc_step), o...]
    dot_general x36 -> x0, matrix products: 23.2 us -> none  [the longest x6 4.88 us: grad_step(): jnp.einsum('hqk,qhd->khd', weights_low, grads_out, preferred_element_type...]
    ppermute x4 -> x0, starting transfers between devices: 14.6 us -> none  [the longest x2 7.29 us: from_behind(): return lax.ppermute(shard, axis, pairs)]
    dynamic_update_slice x6 -> x0, other arithmetic: 8.86 us -> none  [shards(): lax.scan(grad_step, start_query, jnp.arange(n_blocks, dtype=jnp.int32))]
    dynamic_slice x36 -> x0, local copies, waits for them, and re-layouts: 8.67 us -> none  [the longest x12 7.01 us: shards(): lax.scan(stats_step, start_stats, jnp.arange(n_blocks, dtype=jnp.int32))]
    another operation x2 -> x0, loops' own time: 8.55 us -> none  [the longest x1 4.33 us: shards(): lax.scan(stats_step, start_stats, jnp.arange(n_blocks, dtype=jnp.int32))]
  transfers between devices with their start and end apart: 4 -> 0, of which waited for: 2 -> 0; matrix products, arithmetic and copies ran while one was open for 2% -> 0% of each run, Pallas kernels for 0% -> 0%
where the time goes in v1:
time: 40.7 us; the launch traced here: 40.6 us
  Pallas kernels  33.4 us (82%)
  local copies, waits for them, and re-layouts  6.51 us (16%)
  between operations  0.64 us (2%)
    pallas_call x1, Pallas kernels, shards(): pl.pallas_call(functools.partial(kernel, n_seq, n_loc, step, enc_step), o...  33.4 us
    unnamed x5, local copies, waits for them, and re-layouts  6.51 us

profile of v1, /device:TPU:0, one launch (start us, length us, event | category | flops | bytes accessed | tf_op | source)
XLA Modules:
  0.0 40.6 jit_solution(6169561578073264060)
XLA Ops:
  0.6 33.4 %shard_map.94 = (bf16[1,128,2048]{2,1,0:T(8,128)(2,1)}, bf16[1,512,2048]{2,1,0:T(8,128)(2,1)}, bf16[1,512,2048]{2,1,0:T(8,128)(2,1)}) custom-call(s32[1,33]{1,0:T(1,128)} %ds_ref.1, s32[1,33]{1,0:T(1,128)} %es_ref.1, bf16[1,128,2048]{2,1,0:T(8,128)(2,1)} %q_hbm.1, bf16[1,512,2048]{2,1,0:T(8,128)(2,1)} %k_hbm.1, bf16[1,512,2048]{2,1,0:T(8,128)(2,1)} %v_hbm.1, ...), custom_call_target="tpu_custom_call" | custom-call | tf_op jit(solution)/shard_map/pallas_call | solution.py:306
  34.1 1.9 %copy.13 = bf16[1,128,2048]{2,1,0:T(8,128)(2,1)} copy(bf16[1,128,2048]{2,1,0:T(8,128)(2,1)} %get-tuple-element.6) | data formatting | bytes 1048576
  35.9 0.0 copy-start
  35.9 3.3 %copy.14 = bf16[1,512,2048]{2,1,0:T(8,128)(2,1)} copy(bf16[1,512,2048]{2,1,0:T(8,128)(2,1)} %get-tuple-element.7) | data formatting | bytes 4194304
  39.3 0.0 copy-done
  39.3 1.3 %copy.15 = bf16[1,512,2048]{2,1,0:T(8,128)(2,1)} copy(bf16[1,512,2048]{2,1,0:T(8,128)(2,1)S(1)} %copy-done) | data formatting | bytes 4194304
Async XLA Ops:
  35.9 3.3 %copy-start = (bf16[1,512,2048]{2,1,0:T(8,128)(2,1)S(1)}, bf16[1,512,2048]{2,1,0:T(8,128)(2,1)}, u32[]{:S(2)}) copy-start(bf16[1,512,2048]{2,1,0:T(8,128)(2,1)} %get-tuple-element.8) | copy-start | bytes 6291460

commit v2 on v1

--- a/solution.py
+++ b/solution.py
@@ -24,10 +24,10 @@
 def kernel(
     n_seq, n_loc, step, enc_step,
     ds_ref, es_ref, q_hbm, k_hbm, v_hbm, so_hbm, do_hbm,
-    dq_hbm, dk_hbm, dv_hbm,
+    dq_out, dk, dv,
     q, do, so, k, v, xq, xo, bdq, bdo, sbuf, dsb, psb, kid, st, rst_l, rst_r,
-    dq, dqx, rdq_a, rdq_b, dqo, dk, dv,
-    in_sem, snd, rcv, out_sem,
+    dq, dqx, rdq_a, rdq_b,
+    in_sem, snd, rcv,
 ):
     me = lax.axis_index("seq")
     has_left = me > 0
@@ -153,43 +153,61 @@
     def blk(c):
         return pl.ds(c * lanes, lanes)
 
-    def build(g, c, qs, dos):
-        bdq[g, blk(c)] = spread(qs)
-        bdo[g, blk(c)] = spread(dos)
-
-    ones = jnp.ones((8, WIDTH), jnp.bfloat16)
+    sel_at = [lax.broadcasted_iota(jnp.int32, (WIDTH, lanes), n) for n in range(2)]
+    pick = (lax.div(sel_at[0], HD) == lax.div(sel_at[1], step)).astype(jnp.bfloat16)
+    diag_at = [lax.broadcasted_iota(jnp.int32, (step, lanes), n) for n in range(2)]
+    diag = diag_at[0] == lax.rem(diag_at[1], step)
 
     def out_dot(dos, sos):
         w = dos.astype(jnp.float32) * sos.astype(jnp.float32)
         hi = w.astype(jnp.bfloat16)
-        rest = w - hi.astype(jnp.float32)
-        mid = rest.astype(jnp.bfloat16)
-        low = (rest - mid.astype(jnp.float32)).astype(jnp.bfloat16)
-        total = dot(ones, spread(low), NT) + dot(ones, spread(mid), NT) + dot(ones, spread(hi), NT)
-        return total[0:1]
-
-    def scores(g, c):
+        low = (w - hi.astype(jnp.float32)).astype(jnp.bfloat16)
+        total = dot(hi, pick, NN) + dot(low, pick, NN)
+        return jnp.sum(jnp.where(diag, total, 0.0), axis=0, keepdims=True)
+
+    def build(g, cs, qs, dos):
+        bq = [spread(x) for x in qs]
+        bo = [spread(x) for x in dos]
+        for c, x, y in zip(cs, bq, bo):
+            bdq[g, blk(c)] = x
+            bdo[g, blk(c)] = y
+        return bq, bo
+
+    def part(ref, g, c):
         lo, hi = rows_of(c)
-        s = dot(k[lo:hi, cols(g)], bdq[g, blk(c)], NT)
-        s = jnp.where(kid[lo:hi] == qid[c], s, masked_low)
-        m = jnp.max(s, axis=0, keepdims=True)
-        l = jnp.sum(jnp.exp(s - jnp.maximum(m, 0.5 * masked_low)), axis=0, keepdims=True)
-        return s, m, l
-
-    def first_pass(g, c):
-        s, m, l = scores(g, c)
+        return ref[lo:hi, cols(g)]
+
+    def masked_scores(g, cs, bq):
+        raw = [dot(part(k, g, c), x, NT) for c, x in zip(cs, bq)]
+        return [
+            jnp.where(kid[rows_of(c)[0] : rows_of(c)[1]] == qid[c], s, masked_low)
+            for c, s in zip(cs, raw)
+        ]
+
+    def totals(ss):
+        ms = [jnp.max(s, axis=0, keepdims=True) for s in ss]
+        ls = [
+            jnp.sum(jnp.exp(s - jnp.maximum(m, 0.5 * masked_low)), axis=0, keepdims=True)
+            for s, m in zip(ss, ms)
+        ]
+        return ms, ls
+
+    def keep(g, c, s, m, l):
         sbuf[g, pl.ds(s_at[c], s.shape[0])] = s
         st[c, 0, pl.ds(g, 1)] = m
         st[c, 1, pl.ds(g, 1)] = l
 
-    def second_pass(g, c, s, total, od):
-        lo, hi = rows_of(c)
-        p = jnp.exp(s - total)
-        dp = dot(v[lo:hi, cols(g)], bdo[g, blk(c)], NT)
-        dsc = (p * (dp - od)).astype(jnp.bfloat16)
-        psb[g, lo:hi, blk(c)] = p.astype(jnp.bfloat16)
-        dsb[g, lo:hi, blk(c)] = dsc
-        return gather(dot(dsc, k[lo:hi, cols(g)], TN))
+    def grads(g, cs, bo, ss, lts, ods):
+        dps = [dot(part(v, g, c), x, NT) for c, x in zip(cs, bo)]
+        ps = [jnp.exp(s - lt) for s, lt in zip(ss, lts)]
+        dss = [(p * (dp - od)).astype(jnp.bfloat16) for p, dp, od in zip(ps, dps, ods)]
+        turned = [x.T for x in dss]
+        dqs = [dot(x, part(k, g, c), NN) for c, x in zip(cs, turned)]
+        for c, p, x in zip(cs, ps, dss):
+            lo, hi = rows_of(c)
+            psb[g, lo:hi, blk(c)] = p.astype(jnp.bfloat16)
+            dsb[g, lo:hi, blk(c)] = x
+        return [gather(x) for x in dqs]
 
     def own(c):
         return pl.ds((c - 1) * step, step)
@@ -197,82 +215,86 @@
     for c in loads:
         c.wait()
 
-    @pl.loop(0, groups)
+    @pl.loop(0, groups, unroll=4)
     def _(g):
         for j in range(n_loc):
             z = jnp.zeros((enc_step - ehalf, lanes), jnp.bfloat16)
             psb[g, pl.ds(j * enc_step + ehalf, enc_step - ehalf), blk(j)] = z
             dsb[g, pl.ds(j * enc_step + ehalf, enc_step - ehalf), blk(j)] = z
-        for c in range(1, last):
-            dos = do[own(c), cols(g)]
-            build(g, c, q[own(c), cols(g)], dos)
-            od = out_dot(dos, so[own(c), cols(g)])
-            if c in (1, last - 1):
-                first_pass(g, c)
-                st[c, 2, pl.ds(g, 1)] = od
-            else:
-                s, m, l = scores(g, c)
-                dq[own(c), cols(g)] = second_pass(g, c, s, m + jnp.log(l), od)
+        cs = list(range(1, last))
+        doss = [do[own(c), cols(g)] for c in cs]
+        bq, bo = build(g, cs, [q[own(c), cols(g)] for c in cs], doss)
+        ss = masked_scores(g, cs, bq)
+        ods = [out_dot(x, so[own(c), cols(g)]) for c, x in zip(cs, doss)]
+        ms, ls = totals(ss)
+        for n in (0, -1):
+            keep(g, cs[n], ss[n], ms[n], ls[n])
+            st[cs[n], 2, pl.ds(g, 1)] = ods[n]
+        inner = cs[1:-1]
+        lts = [m + jnp.log(l) for m, l in zip(ms[1:-1], ls[1:-1])]
+        for c, x in zip(inner, grads(g, inner, bo[1:-1], ss[1:-1], lts, ods[1:-1])):
+            dq[own(c), cols(g)] = x
 
     arrived((0, 1))
 
-    @pl.loop(0, groups)
-    def _(g):
-        for c in (0, last):
-            r = pl.ds(0 if c == 0 else step, step)
-            build(g, c, xq[r, cols(g)], xo[r, cols(g)])
-            first_pass(g, c)
-            st[c, 2, pl.ds(g, 1)] = jnp.zeros((1, lanes), jnp.float32)
+    @pl.loop(0, groups, unroll=4)
+    def _(g):
+        cs = (0, last)
+        both = [pl.ds(0, step), pl.ds(step, step)]
+        bq, bo = build(g, cs, [xq[r, cols(g)] for r in both], [xo[r, cols(g)] for r in both])
+        ss = masked_scores(g, cs, bq)
+        ms, ls = totals(ss)
+        for n in range(2):
+            keep(g, cs[n], ss[n], ms[n], ls[n])
+            st[cs[n], 2, pl.ds(g, 1)] = jnp.zeros((1, lanes), jnp.float32)
 
     start((2,))
     arrived((2,))
 
-    def finish(g, c, other, od_ref):
+    def finish(g, cs, others, od_refs):
         row = pl.ds(g, 1)
-        m1, m2 = st[c, 0, row], other[0, row]
-        l1, l2 = st[c, 1, row], other[1, row]
-        m = jnp.maximum(m1, m2)
-        l = l1 * jnp.exp(m1 - m) + l2 * jnp.exp(m2 - m)
-        total = jnp.where(l > 0.0, m + jnp.log(l), 0.0)
-        lo, hi = rows_of(c)
-        s = sbuf[g, pl.ds(s_at[c], hi - lo)]
-        return second_pass(g, c, s, total, od_ref[2, row])
-
-    @pl.loop(0, groups)
-    def _(g):
-        dqx[pl.ds(0, step), cols(g)] = finish(
-            g, 0, rst_l.at[0], rst_l.at[0]).astype(jnp.bfloat16)
-        dqx[pl.ds(step, step), cols(g)] = finish(
-            g, last, rst_r.at[1], rst_r.at[1]).astype(jnp.bfloat16)
+        ss, lts = [], []
+        for c, other in zip(cs, others):
+            m1, m2 = st[c, 0, row], other[0, row]
+            l1, l2 = st[c, 1, row], other[1, row]
+            m = jnp.maximum(m1, m2)
+            l = l1 * jnp.exp(m1 - m) + l2 * jnp.exp(m2 - m)
+            lts.append(jnp.where(l > 0.0, m + jnp.log(l), 0.0))
+            lo, hi = rows_of(c)
+            ss.append(sbuf[g, pl.ds(s_at[c], hi - lo)])
+        bo = [bdo[g, blk(c)] for c in cs]
+        return grads(g, cs, bo, ss, lts, [r[2, row] for r in od_refs])
+
+    edges = (rst_l.at[0], rst_r.at[1])
+
+    @pl.loop(0, groups, unroll=4)
+    def _(g):
+        a, z = finish(g, (0, last), edges, edges)
+        dqx[pl.ds(0, step), cols(g)] = a.astype(jnp.bfloat16)
+        dqx[pl.ds(step, step), cols(g)] = z.astype(jnp.bfloat16)
 
     start((3,))
 
-    outs = []
-    @pl.loop(0, groups)
-    def _(g):
-        dq[own(1), cols(g)] = finish(g, 1, rst_l.at[1], st.at[1])
-        dq[own(last - 1), cols(g)] = finish(g, last - 1, rst_r.at[0], st.at[last - 1])
+    @pl.loop(0, groups, unroll=4)
+    def _(g):
+        a, z = finish(
+            g, (1, last - 1), (rst_l.at[1], rst_r.at[0]), (st.at[1], st.at[last - 1])
+        )
+        dq[own(1), cols(g)] = a
+        dq[own(last - 1), cols(g)] = z
+
+    @pl.loop(0, groups, unroll=4)
+    def _(g):
         for j in range(n_loc):
             rows = pl.ds(j * enc_step, enc_step)
             span = pl.ds(j * lanes, 3 * lanes)
-            dk[rows, cols(g)] = dot(dsb[g, rows, span], bdq[g, span], NN).astype(jnp.bfloat16)
-            dv[rows, cols(g)] = dot(psb[g, rows, span], bdo[g, span], NN).astype(jnp.bfloat16)
-        pltpu.make_async_copy(dk.at[:, cols(g)], dk_hbm.at[0, :, cols(g)], out_sem.at[0, g]).start()
-        pltpu.make_async_copy(dv.at[:, cols(g)], dv_hbm.at[0, :, cols(g)], out_sem.at[1, g]).start()
+            dk[0, rows, cols(g)] = dot(dsb[g, rows, span], bdq[g, span], NN).astype(jnp.bfloat16)
+            dv[0, rows, cols(g)] = dot(psb[g, rows, span], bdo[g, span], NN).astype(jnp.bfloat16)
 
     arrived((3,))
     dq[pl.ds(0, half)] = dq[pl.ds(0, half)] + rdq_a[...].astype(jnp.float32)
     dq[tail] = dq[tail] + rdq_b[...].astype(jnp.float32)
-    dqo[...] = dq[...].astype(jnp.bfloat16)
-    fin = pltpu.make_async_copy(dqo, dq_hbm.at[0], in_sem.at[0])
-    fin.start()
-
-    @pl.loop(0, groups)
-    def _(g):
-        pltpu.make_async_copy(dk.at[:, cols(g)], dk_hbm.at[0, :, cols(g)], out_sem.at[0, g]).wait()
-        pltpu.make_async_copy(dv.at[:, cols(g)], dv_hbm.at[0, :, cols(g)], out_sem.at[1, g]).wait()
-
-    fin.wait()
+    dq_out[0] = dq[...].astype(jnp.bfloat16)
 
     def sent_right():
         for c in to_right:
@@ -302,16 +324,17 @@
     bf, f32 = jnp.bfloat16, jnp.float32
     vm = pltpu.VMEM
     hbm = pl.BlockSpec(memory_space=pl.ANY)
+    vmem = pl.BlockSpec(memory_space=vm)
     smem = pl.BlockSpec(memory_space=pltpu.SMEM)
     return pl.pallas_call(
         functools.partial(kernel, n_seq, n_loc, step, enc_step),
         out_shape=(
-            jax.ShapeDtypeStruct(dec_query.shape, bf),
-            jax.ShapeDtypeStruct(enc_key.shape, bf),
-            jax.ShapeDtypeStruct(enc_value.shape, bf),
+            vm(dec_query.shape, bf),
+            vm(enc_key.shape, bf),
+            vm(enc_value.shape, bf),
         ),
         in_specs=[smem, smem] + [hbm] * 5,
-        out_specs=(hbm, hbm, hbm),
+        out_specs=(vmem, vmem, vmem),
         scratch_shapes=[
             vm((q_rows, width), bf), vm((q_rows, width), bf), vm((q_rows, width), bf),
             vm((k_rows, width), bf), vm((k_rows, width), bf),
@@ -323,14 +346,12 @@
             vm((chunks, 3, groups, lanes), f32),
             vm((2, 3, groups, lanes), f32), vm((2, 3, groups, lanes), f32),
             vm((q_rows, width), f32), vm((2 * step, width), bf),
-            vm((half, width), bf), vm((step, width), bf), vm((q_rows, width), bf),
-            vm((k_rows, width), bf), vm((k_rows, width), bf),
+            vm((half, width), bf), vm((step, width), bf),
             pltpu.SemaphoreType.DMA((5,)),
             pltpu.SemaphoreType.DMA((8,)), pltpu.SemaphoreType.DMA((8,)),
-            pltpu.SemaphoreType.DMA((2, groups)),
         ],
         compiler_params=pltpu.CompilerParams(
-            collective_id=0, has_side_effects=True, vmem_limit_bytes=56 * 1024 * 1024
+            collective_id=0, has_side_effects=True, vmem_limit_bytes=48 * 1024 * 1024
         ),
     )(dec_start, enc_start, dec_query, enc_key, enc_value, saved_out, d_out)
 

time: 40.7 us -> 32.6 us (0.80)
  Pallas kernels: 33.4 us -> 24.9 us
    pallas_call x1, Pallas kernels: 33.4 us -> 24.9 us  [shards(): pl.pallas_call(functools.partial(kernel, n_seq, n_loc, step, enc_step), o...]
    unnamed x5 -> x11, local copies, waits for them, and re-layouts: 6.51 us -> 6.82 us
where the time goes in v2:
time: 32.6 us; the launch traced here: 32.4 us
  Pallas kernels  24.9 us (76%)
  local copies, waits for them, and re-layouts  6.82 us (21%)
  between operations  0.65 us (2%)
    pallas_call x1, Pallas kernels, shards(): pl.pallas_call(functools.partial(kernel, n_seq, n_loc, step, enc_step), o...  24.9 us
    unnamed x11, local copies, waits for them, and re-layouts  6.82 us

profile of v2, /device:TPU:0, one launch (start us, length us, event | category | flops | bytes accessed | tf_op | source)
XLA Modules:
  0.0 32.4 jit_solution(6996406305270459754)
XLA Ops:
  0.6 0.0 copy-start
  0.6 1.0 %copy-done = bf16[1,128,2048]{2,1,0:T(8,128)(2,1)S(1)} copy-done((bf16[1,128,2048]{2,1,0:T(8,128)(2,1)S(1)}, bf16[1,128,2048]{2,1,0:T(8,128)(2,1)}, u32[]{:S(2)}) %copy-start) | copy-done | bytes 524312
  1.7 0.0 copy-start.1
  1.7 1.0 %copy-done.1 = bf16[1,128,2048]{2,1,0:T(8,128)(2,1)S(1)} copy-done((bf16[1,128,2048]{2,1,0:T(8,128)(2,1)S(1)}, bf16[1,128,2048]{2,1,0:T(8,128)(2,1)}, u32[]{:S(2)}) %copy-start.1) | copy-done | bytes 524312
  2.7 0.0 copy-start.2
  2.7 0.7 %copy-done.2 = s32[1,33]{1,0:T(1,128)S(1)} copy-done((s32[1,33]{1,0:T(1,128)S(1)}, s32[1,33]{1,0:T(1,128)}, u32[]{:S(2)}) %copy-start.2) | copy-done | bytes 156
  3.4 0.0 copy-start.3
  3.4 0.7 %copy-done.3 = s32[1,33]{1,0:T(1,128)S(1)} copy-done((s32[1,33]{1,0:T(1,128)S(1)}, s32[1,33]{1,0:T(1,128)}, u32[]{:S(2)}) %copy-start.3) | copy-done | bytes 156
  4.0 24.9 %shard_map.94 = (bf16[1,128,2048]{2,1,0:T(8,128)(2,1)S(1)}, bf16[1,512,2048]{2,1,0:T(8,128)(2,1)S(1)}, bf16[1,512,2048]{2,1,0:T(8,128)(2,1)S(1)}) custom-call(s32[1,33]{1,0:T(1,128)S(1)} %copy-done.2, s32[1,33]{1,0:T(1,128)S(1)} %copy-done.3, bf16[1,128,2048]{2,1,0:T(8,128)(2,1)S(1)} %copy-done, bf16[1,512,2048]{2,1,0:T(8,128)(2,1)} %k_hbm.1, ...), custom_call_target="tpu_custom_call" | custom-call | tf_op jit(solution)/shard_map/pallas_call | solution.py:329
  28.9 0.8 %copy.13 = bf16[1,128,2048]{2,1,0:T(8,128)(2,1)} copy(bf16[1,128,2048]{2,1,0:T(8,128)(2,1)S(1)} %get-tuple-element.3) | data formatting | bytes 1048576
  29.7 1.3 %copy.14 = bf16[1,512,2048]{2,1,0:T(8,128)(2,1)} copy(bf16[1,512,2048]{2,1,0:T(8,128)(2,1)S(1)} %get-tuple-element.4) | data formatting | bytes 4194304
  31.1 1.3 %copy.15 = bf16[1,512,2048]{2,1,0:T(8,128)(2,1)} copy(bf16[1,512,2048]{2,1,0:T(8,128)(2,1)S(1)} %get-tuple-element.5) | data formatting | bytes 4194304
Async XLA Ops:
  0.6 1.0 %copy-start = (bf16[1,128,2048]{2,1,0:T(8,128)(2,1)S(1)}, bf16[1,128,2048]{2,1,0:T(8,128)(2,1)}, u32[]{:S(2)}) copy-start(bf16[1,128,2048]{2,1,0:T(8,128)(2,1)} %q_hbm.1) | copy-start | bytes 1572868
  1.7 1.0 %copy-start.1 = (bf16[1,128,2048]{2,1,0:T(8,128)(2,1)S(1)}, bf16[1,128,2048]{2,1,0:T(8,128)(2,1)}, u32[]{:S(2)}) copy-start(bf16[1,128,2048]{2,1,0:T(8,128)(2,1)} %so_hbm.1) | copy-start | bytes 1572868
  2.7 0.7 %copy-start.2 = (s32[1,33]{1,0:T(1,128)S(1)}, s32[1,33]{1,0:T(1,128)}, u32[]{:S(2)}) copy-start(s32[1,33]{1,0:T(1,128)} %ds_ref.1) | copy-start | bytes 400
  3.4 0.7 %copy-start.3 = (s32[1,33]{1,0:T(1,128)S(1)}, s32[1,33]{1,0:T(1,128)}, u32[]{:S(2)}) copy-start(s32[1,33]{1,0:T(1,128)} %es_ref.1) | copy-start | bytes 400
